TPU v7x, 512 devices: a whole 4x8x8 slice. The times are simulated.
512 devices in a mesh: ctx: 32 (over z, x), head: 16 (over y, core).
Axes of the slice: x: 4, y: 8, z: 8, core: 2. Of those that a mesh axis runs over, the one named last changes fastest.
Arguments:
- query_proj: bfloat16 [16384, 8192], P('ctx', 'head'), may hold values from -90 to 90
- key_value: bfloat16 [16384, 2048], P('ctx', 'head'), may hold values from -90 to 90
- query_gain: float32 [128], replicated, may hold values from 0.25 to 1.75
- key_gain: float32 [128], replicated, may hold values from 0.25 to 1.75
- doc_offsets: int32 [65], replicated, may hold values from 0 to 16384, as said below
Outputs:
- attention: bfloat16 [16384, 8192], P('ctx', 'head')
Inputs may be any that keep to these rules, and one draw needn't show every extreme that they name: `doc_offsets`: entry 0 is 0 and the last is 16384; entries never fall; each difference of neighbours is 0 or a multiple of 256 from 256 to 8448, the nonzero ones first, and one difference equals 8448.
All inputs are finite; a program needn't handle non-finite values.
Results may differ from a plain program's by a relative error of at most 0.0061.
Values may be sent and summed in bfloat16 or wider, within the bound.
A program may use at most 64 MiB of HBM per device.

v0:
```python
import jax
import jax.numpy as jnp
from jax import lax
from jax.sharding import PartitionSpec as P

norm_eps = 1e-06
rope_base = 1000000.0


def from_partner(block, axis, stride):
    count = lax.axis_size(axis)
    route = []
    for low in range(count):
        high = low | 1 << stride
        if high != low and high < count:
            route += [(low, high), (high, low)]
    return lax.ppermute(block, axis, route)


def doc_starts(places, doc_offsets):
    earlier = doc_offsets[None, :] <= places[:, None]
    return jnp.max(jnp.where(earlier, doc_offsets[None, :], 0), axis=1)


def rope_tables(relative, head_width):
    halves = head_width // 2
    exponent = jnp.arange(halves, dtype=jnp.float32) * (2.0 / head_width)
    frequency = jnp.exp(-exponent * jnp.log(jnp.float32(rope_base)))
    angles = relative.astype(jnp.float32)[:, None] * frequency[None, :]
    return (jnp.cos(angles), jnp.sin(angles))


def normed_rotated(projected, gain_vector, cos_table, sin_table):
    halves = projected.shape[-1] // 2
    mean_square = jnp.mean(projected * projected, axis=-1, keepdims=True)
    scaled = projected * lax.rsqrt(mean_square + norm_eps) * gain_vector
    first_half = scaled[..., :halves]
    second_half = scaled[..., halves:]
    cos_rows = cos_table[:, None, :]
    sin_rows = sin_table[:, None, :]
    return jnp.concatenate(
        [
            first_half * cos_rows - second_half * sin_rows,
            second_half * cos_rows + first_half * sin_rows,
        ],
        axis=-1,
    )


def attend_block(running, row_data, key_block, value_block, key_start):
    query_rows, row_places, row_starts = row_data
    key_count = key_block.shape[0]
    key_places = key_start + jnp.arange(key_count, dtype=jnp.int32)

    def per_rows(item_data):
        query_part, place_part, start_part, numer_part, denom_part = item_data
        touched = jnp.logical_and(
            key_start <= jnp.max(place_part), key_start + key_count - 1 >= jnp.min(start_part)
        )

        def compute(totals):
            numer_total, denom_total = totals
            scores = jnp.einsum(
                "rhd,kd->rhk", query_part, key_block, preferred_element_type=jnp.float32
            )
            allowed = jnp.logical_and(
                key_places[None, :] <= place_part[:, None],
                key_places[None, :] >= start_part[:, None],
            )
            weights = jnp.where(allowed[:, None, :], jnp.exp(scores), 0.0)
            denom_total = denom_total + jnp.sum(weights, axis=-1)
            numer_total = numer_total + jnp.einsum(
                "rhk,kd->rhd",
                weights.astype(jnp.bfloat16),
                value_block,
                preferred_element_type=jnp.float32,
            )
            return (numer_total, denom_total)

        def unchanged(totals):
            return totals

        return lax.cond(touched, compute, unchanged, (numer_part, denom_part))

    return lax.map(per_rows, (query_rows, row_places, row_starts, running[0], running[1]))


def attend_span(running, row_data, key_rows, value_rows, block_rows):
    block_count = key_rows.shape[0] // block_rows
    key_parts = key_rows.reshape(block_count, block_rows, key_rows.shape[-1])
    value_parts = value_rows.reshape(block_count, block_rows, value_rows.shape[-1])

    def one_block(partial_value, item_data):
        key_part, value_part, position = item_data
        return (
            attend_block(partial_value, row_data, key_part, value_part, position * block_rows),
            None,
        )

    result, _ = lax.scan(
        one_block, running, (key_parts, value_parts, jnp.arange(block_count, dtype=jnp.int32))
    )
    return result


def per_device(query_proj, key_value, query_gain, key_gain, doc_offsets):
    local_rows = query_proj.shape[0]
    head_width = query_gain.shape[0]
    local_heads = query_proj.shape[1] // head_width
    context_index = lax.axis_index("ctx")
    head_index = lax.axis_index("head")
    block_rows = min(local_rows, 512)
    places = context_index * local_rows + jnp.arange(local_rows, dtype=jnp.int32)
    starts = doc_starts(places, doc_offsets)
    cos_table, sin_table = rope_tables(places - starts, head_width)
    projected = query_proj.astype(jnp.float32).reshape(local_rows, local_heads, head_width)
    queries = (
        normed_rotated(projected, query_gain, cos_table, sin_table) * head_width ** (-0.5)
    ).astype(jnp.bfloat16)
    rotated = normed_rotated(
        key_value.astype(jnp.float32)[:, None, :], key_gain, cos_table, sin_table
    )[:, 0, :].astype(jnp.bfloat16)
    holds_key = head_index % 2 == 0
    outgoing = jnp.where(holds_key, rotated, key_value)
    incoming = from_partner(outgoing, "head", 0)
    key_rows = jnp.where(holds_key, outgoing, incoming)
    value_rows = jnp.where(holds_key, incoming, outgoing)
    block_count = local_rows // block_rows
    row_data = (
        queries.reshape(block_count, block_rows, local_heads, head_width),
        places.reshape(block_count, block_rows),
        starts.reshape(block_count, block_rows),
    )
    running_sums = (
        jnp.zeros((block_count, block_rows, local_heads, head_width), jnp.float32),
        jnp.zeros((block_count, block_rows, local_heads), jnp.float32),
    )
    running_sums = attend_span(
        running_sums,
        row_data,
        lax.all_gather(key_rows, "ctx", axis=0, tiled=True),
        lax.all_gather(value_rows, "ctx", axis=0, tiled=True),
        local_rows,
    )
    numerator, denominator = running_sums
    mixed = (
        (numerator / denominator[..., None])
        .astype(jnp.bfloat16)
        .reshape(local_rows, local_heads * head_width)
    )
    return mixed


def solution(mesh):
    placed = (P("ctx", "head"), P("ctx", "head"), P(), P(), P())
    return jax.shard_map(
        per_device, mesh=mesh, in_specs=placed, out_specs=P("ctx", "head"), check_vma=False
    )
```

profile of v0, /device:TPU:468, one launch (start us, length us, event | category | flops | bytes accessed | tf_op | source)
XLA Modules:
  0.0 369.2 jit_solution(3883186642300603758)
XLA Ops:
  6.6 0.8 select_reduce_fusion
  8.0 1.0 copy.17
  9.1 0.7 fusion.28
  10.5 1.9 collective-permute-start
  12.4 1.3 collective-permute-done
  15.2 1.3 copy.19
  17.9 0.7 add_reduce_fusion
  18.7 84.9 %all-gather.3.cloned.1.call-done = bf16[16384,128]{0,1:T(8,128)(2,1)} async-done(((bf16[512,128]{0,1:T(8,128)(2,1)}), bf16[16384,128]{0,1:T(8,128)(2,1)}) %all-gather.3.cloned.1.call-update) | async-done | bytes 4194320 | tf_op jit(solution)/shard_map/all_gather | solution.py:141
  103.5 6.4 %copy.25 = bf16[16384,128]{1,0:T(8,128)(2,1)} copy(bf16[16384,128]{0,1:T(8,128)(2,1)} %all-gather.3.cloned.1.call-done) | data formatting | bytes 8388608
  109.9 86.1 %all-gather.5.cloned.1.call-done = bf16[16384,128]{0,1:T(8,128)(2,1)} async-done(((bf16[512,128]{0,1:T(8,128)(2,1)}), bf16[16384,128]{0,1:T(8,128)(2,1)}) %all-gather.5.cloned.1.call-update) | async-done | bytes 4194320 | tf_op jit(solution)/shard_map/all_gather | solution.py:142
  196.0 6.4 %copy.26 = bf16[16384,128]{1,0:T(8,128)(2,1)} copy(bf16[16384,128]{0,1:T(8,128)(2,1)} %all-gather.5.cloned.1.call-done) | data formatting | bytes 8388608
  202.5 158.3 %while.22 = (s32[]{:T(128)}, f32[1,512,4,128]{3,1,2,0:T(8,128)S(1)}, f32[1,512,4]{1,2,0:T(4,128)S(1)}, s32[32]{0:T(128)S(1)}, s32[]{:T(128)}, /*index=5*/s32[]{:...) while((s32[]{:T(128)}, ...), condition=%wide.region_9.10_spmd.clone, body=%wide.region_5.9_spmd.clone.sunk | while | flops 542114816 | bytes 12111171 | solution.py:100
  241.6 4.4 %conditional.3 = (f32[1,512,4,128]{3,1,2,0:T(8,128)S(1)}, f32[1,512,4]{1,2,0:T(4,128)S(1)}) conditional(s32[]{:T(128)} %convert_element_type.67, (f32[512,4,128]{2,0,1:T(8,128)S(1)}, f32[512,4]{0,1:T(4,128)S(1)}) %tuple.90, (s32[]{:T(128)}, s32[512]{0:T(512)S(1)}, s32[]{:T(128)}, s32[1,512]{1,0:T(1,128)S(1)}, bf16[32,512,128]{2,1,0:T(8,128)(2,1)}, ...), branch_computations={%region_6.6_spmd, %region_7.8_spmd} | conditional | flops 542114816 | bytes 12106776 | solution.py:83
  241.9 1.9 fusion.2
  243.8 2.1 fusion.11
  248.6 4.4 %conditional.3 = (f32[1,512,4,128]{3,1,2,0:T(8,128)S(1)}, f32[1,512,4]{1,2,0:T(4,128)S(1)}) conditional(s32[]{:T(128)} %convert_element_type.67, (f32[512,4,128]{2,0,1:T(8,128)S(1)}, f32[512,4]{0,1:T(4,128)S(1)}) %tuple.90, (s32[]{:T(128)}, s32[512]{0:T(512)S(1)}, s32[]{:T(128)}, s32[1,512]{1,0:T(1,128)S(1)}, bf16[32,512,128]{2,1,0:T(8,128)(2,1)}, ...), branch_computations={%region_6.6_spmd, %region_7.8_spmd} | conditional | flops 542114816 | bytes 12106776 | solution.py:83
  248.9 1.9 fusion.2
  250.8 2.1 fusion.11
  255.6 4.4 %conditional.3 = (f32[1,512,4,128]{3,1,2,0:T(8,128)S(1)}, f32[1,512,4]{1,2,0:T(4,128)S(1)}) conditional(s32[]{:T(128)} %convert_element_type.67, (f32[512,4,128]{2,0,1:T(8,128)S(1)}, f32[512,4]{0,1:T(4,128)S(1)}) %tuple.90, (s32[]{:T(128)}, s32[512]{0:T(512)S(1)}, s32[]{:T(128)}, s32[1,512]{1,0:T(1,128)S(1)}, bf16[32,512,128]{2,1,0:T(8,128)(2,1)}, ...), branch_computations={%region_6.6_spmd, %region_7.8_spmd} | conditional | flops 542114816 | bytes 12106776 | solution.py:83
  255.9 1.9 fusion.2
  257.9 2.1 fusion.11
  262.6 4.4 %conditional.3 = (f32[1,512,4,128]{3,1,2,0:T(8,128)S(1)}, f32[1,512,4]{1,2,0:T(4,128)S(1)}) conditional(s32[]{:T(128)} %convert_element_type.67, (f32[512,4,128]{2,0,1:T(8,128)S(1)}, f32[512,4]{0,1:T(4,128)S(1)}) %tuple.90, (s32[]{:T(128)}, s32[512]{0:T(512)S(1)}, s32[]{:T(128)}, s32[1,512]{1,0:T(1,128)S(1)}, bf16[32,512,128]{2,1,0:T(8,128)(2,1)}, ...), branch_computations={%region_6.6_spmd, %region_7.8_spmd} | conditional | flops 542114816 | bytes 12106776 | solution.py:83
  262.9 1.9 fusion.2
  264.9 2.1 fusion.11
  269.6 4.4 %conditional.3 = (f32[1,512,4,128]{3,1,2,0:T(8,128)S(1)}, f32[1,512,4]{1,2,0:T(4,128)S(1)}) conditional(s32[]{:T(128)} %convert_element_type.67, (f32[512,4,128]{2,0,1:T(8,128)S(1)}, f32[512,4]{0,1:T(4,128)S(1)}) %tuple.90, (s32[]{:T(128)}, s32[512]{0:T(512)S(1)}, s32[]{:T(128)}, s32[1,512]{1,0:T(1,128)S(1)}, bf16[32,512,128]{2,1,0:T(8,128)(2,1)}, ...), branch_computations={%region_6.6_spmd, %region_7.8_spmd} | conditional | flops 542114816 | bytes 12106776 | solution.py:83
  269.9 1.9 fusion.2
  271.9 2.1 fusion.11
  276.6 4.4 %conditional.3 = (f32[1,512,4,128]{3,1,2,0:T(8,128)S(1)}, f32[1,512,4]{1,2,0:T(4,128)S(1)}) conditional(s32[]{:T(128)} %convert_element_type.67, (f32[512,4,128]{2,0,1:T(8,128)S(1)}, f32[512,4]{0,1:T(4,128)S(1)}) %tuple.90, (s32[]{:T(128)}, s32[512]{0:T(512)S(1)}, s32[]{:T(128)}, s32[1,512]{1,0:T(1,128)S(1)}, bf16[32,512,128]{2,1,0:T(8,128)(2,1)}, ...), branch_computations={%region_6.6_spmd, %region_7.8_spmd} | conditional | flops 542114816 | bytes 12106776 | solution.py:83
  277.0 1.9 fusion.2
  278.9 2.1 fusion.11
  283.6 4.4 %conditional.3 = (f32[1,512,4,128]{3,1,2,0:T(8,128)S(1)}, f32[1,512,4]{1,2,0:T(4,128)S(1)}) conditional(s32[]{:T(128)} %convert_element_type.67, (f32[512,4,128]{2,0,1:T(8,128)S(1)}, f32[512,4]{0,1:T(4,128)S(1)}) %tuple.90, (s32[]{:T(128)}, s32[512]{0:T(512)S(1)}, s32[]{:T(128)}, s32[1,512]{1,0:T(1,128)S(1)}, bf16[32,512,128]{2,1,0:T(8,128)(2,1)}, ...), branch_computations={%region_6.6_spmd, %region_7.8_spmd} | conditional | flops 542114816 | bytes 12106776 | solution.py:83
  284.0 1.9 fusion.2
  285.9 2.1 fusion.11
  290.6 4.4 %conditional.3 = (f32[1,512,4,128]{3,1,2,0:T(8,128)S(1)}, f32[1,512,4]{1,2,0:T(4,128)S(1)}) conditional(s32[]{:T(128)} %convert_element_type.67, (f32[512,4,128]{2,0,1:T(8,128)S(1)}, f32[512,4]{0,1:T(4,128)S(1)}) %tuple.90, (s32[]{:T(128)}, s32[512]{0:T(512)S(1)}, s32[]{:T(128)}, s32[1,512]{1,0:T(1,128)S(1)}, bf16[32,512,128]{2,1,0:T(8,128)(2,1)}, ...), branch_computations={%region_6.6_spmd, %region_7.8_spmd} | conditional | flops 542114816 | bytes 12106776 | solution.py:83
  291.0 1.9 fusion.2
  292.9 2.1 fusion.11
  297.7 4.4 %conditional.3 = (f32[1,512,4,128]{3,1,2,0:T(8,128)S(1)}, f32[1,512,4]{1,2,0:T(4,128)S(1)}) conditional(s32[]{:T(128)} %convert_element_type.67, (f32[512,4,128]{2,0,1:T(8,128)S(1)}, f32[512,4]{0,1:T(4,128)S(1)}) %tuple.90, (s32[]{:T(128)}, s32[512]{0:T(512)S(1)}, s32[]{:T(128)}, s32[1,512]{1,0:T(1,128)S(1)}, bf16[32,512,128]{2,1,0:T(8,128)(2,1)}, ...), branch_computations={%region_6.6_spmd, %region_7.8_spmd} | conditional | flops 542114816 | bytes 12106776 | solution.py:83
  298.0 1.9 fusion.2
  299.9 2.1 fusion.11
  304.7 4.4 %conditional.3 = (f32[1,512,4,128]{3,1,2,0:T(8,128)S(1)}, f32[1,512,4]{1,2,0:T(4,128)S(1)}) conditional(s32[]{:T(128)} %convert_element_type.67, (f32[512,4,128]{2,0,1:T(8,128)S(1)}, f32[512,4]{0,1:T(4,128)S(1)}) %tuple.90, (s32[]{:T(128)}, s32[512]{0:T(512)S(1)}, s32[]{:T(128)}, s32[1,512]{1,0:T(1,128)S(1)}, bf16[32,512,128]{2,1,0:T(8,128)(2,1)}, ...), branch_computations={%region_6.6_spmd, %region_7.8_spmd} | conditional | flops 542114816 | bytes 12106776 | solution.py:83
  305.0 1.9 fusion.2
  306.9 2.1 fusion.11
  311.7 4.4 %conditional.3 = (f32[1,512,4,128]{3,1,2,0:T(8,128)S(1)}, f32[1,512,4]{1,2,0:T(4,128)S(1)}) conditional(s32[]{:T(128)} %convert_element_type.67, (f32[512,4,128]{2,0,1:T(8,128)S(1)}, f32[512,4]{0,1:T(4,128)S(1)}) %tuple.90, (s32[]{:T(128)}, s32[512]{0:T(512)S(1)}, s32[]{:T(128)}, s32[1,512]{1,0:T(1,128)S(1)}, bf16[32,512,128]{2,1,0:T(8,128)(2,1)}, ...), branch_computations={%region_6.6_spmd, %region_7.8_spmd} | conditional | flops 542114816 | bytes 12106776 | solution.py:83
  312.0 1.9 fusion.2
  313.9 2.1 fusion.11
  318.7 4.4 %conditional.3 = (f32[1,512,4,128]{3,1,2,0:T(8,128)S(1)}, f32[1,512,4]{1,2,0:T(4,128)S(1)}) conditional(s32[]{:T(128)} %convert_element_type.67, (f32[512,4,128]{2,0,1:T(8,128)S(1)}, f32[512,4]{0,1:T(4,128)S(1)}) %tuple.90, (s32[]{:T(128)}, s32[512]{0:T(512)S(1)}, s32[]{:T(128)}, s32[1,512]{1,0:T(1,128)S(1)}, bf16[32,512,128]{2,1,0:T(8,128)(2,1)}, ...), branch_computations={%region_6.6_spmd, %region_7.8_spmd} | conditional | flops 542114816 | bytes 12106776 | solution.py:83
  319.0 1.9 fusion.2
  320.9 2.1 fusion.11
  325.7 4.4 %conditional.3 = (f32[1,512,4,128]{3,1,2,0:T(8,128)S(1)}, f32[1,512,4]{1,2,0:T(4,128)S(1)}) conditional(s32[]{:T(128)} %convert_element_type.67, (f32[512,4,128]{2,0,1:T(8,128)S(1)}, f32[512,4]{0,1:T(4,128)S(1)}) %tuple.90, (s32[]{:T(128)}, s32[512]{0:T(512)S(1)}, s32[]{:T(128)}, s32[1,512]{1,0:T(1,128)S(1)}, bf16[32,512,128]{2,1,0:T(8,128)(2,1)}, ...), branch_computations={%region_6.6_spmd, %region_7.8_spmd} | conditional | flops 542114816 | bytes 12106776 | solution.py:83
  326.0 1.9 fusion.2
  327.9 2.1 fusion.11
  332.7 4.4 %conditional.3 = (f32[1,512,4,128]{3,1,2,0:T(8,128)S(1)}, f32[1,512,4]{1,2,0:T(4,128)S(1)}) conditional(s32[]{:T(128)} %convert_element_type.67, (f32[512,4,128]{2,0,1:T(8,128)S(1)}, f32[512,4]{0,1:T(4,128)S(1)}) %tuple.90, (s32[]{:T(128)}, s32[512]{0:T(512)S(1)}, s32[]{:T(128)}, s32[1,512]{1,0:T(1,128)S(1)}, bf16[32,512,128]{2,1,0:T(8,128)(2,1)}, ...), branch_computations={%region_6.6_spmd, %region_7.8_spmd} | conditional | flops 542114816 | bytes 12106776 | solution.py:83
  333.0 1.9 fusion.2
  334.9 2.1 fusion.11
  339.7 4.4 %conditional.3 = (f32[1,512,4,128]{3,1,2,0:T(8,128)S(1)}, f32[1,512,4]{1,2,0:T(4,128)S(1)}) conditional(s32[]{:T(128)} %convert_element_type.67, (f32[512,4,128]{2,0,1:T(8,128)S(1)}, f32[512,4]{0,1:T(4,128)S(1)}) %tuple.90, (s32[]{:T(128)}, s32[512]{0:T(512)S(1)}, s32[]{:T(128)}, s32[1,512]{1,0:T(1,128)S(1)}, bf16[32,512,128]{2,1,0:T(8,128)(2,1)}, ...), branch_computations={%region_6.6_spmd, %region_7.8_spmd} | conditional | flops 542114816 | bytes 12106776 | solution.py:83
  340.0 1.9 fusion.2
  341.9 2.1 fusion.11
  346.7 4.4 %conditional.3 = (f32[1,512,4,128]{3,1,2,0:T(8,128)S(1)}, f32[1,512,4]{1,2,0:T(4,128)S(1)}) conditional(s32[]{:T(128)} %convert_element_type.67, (f32[512,4,128]{2,0,1:T(8,128)S(1)}, f32[512,4]{0,1:T(4,128)S(1)}) %tuple.90, (s32[]{:T(128)}, s32[512]{0:T(512)S(1)}, s32[]{:T(128)}, s32[1,512]{1,0:T(1,128)S(1)}, bf16[32,512,128]{2,1,0:T(8,128)(2,1)}, ...), branch_computations={%region_6.6_spmd, %region_7.8_spmd} | conditional | flops 542114816 | bytes 12106776 | solution.py:83
  347.0 1.9 fusion.2
  348.9 2.1 fusion.11
  353.7 4.4 %conditional.3 = (f32[1,512,4,128]{3,1,2,0:T(8,128)S(1)}, f32[1,512,4]{1,2,0:T(4,128)S(1)}) conditional(s32[]{:T(128)} %convert_element_type.67, (f32[512,4,128]{2,0,1:T(8,128)S(1)}, f32[512,4]{0,1:T(4,128)S(1)}) %tuple.90, (s32[]{:T(128)}, s32[512]{0:T(512)S(1)}, s32[]{:T(128)}, s32[1,512]{1,0:T(1,128)S(1)}, bf16[32,512,128]{2,1,0:T(8,128)(2,1)}, ...), branch_computations={%region_6.6_spmd, %region_7.8_spmd} | conditional | flops 542114816 | bytes 12106776 | solution.py:83
  354.0 1.9 fusion.2
  355.9 2.1 fusion.11
  361.5 0.9 copy.29
  (205 shorter events, 29.2 us)
Async XLA Ops:
  6.5 10.6 %copy-start = (f32[128]{0:T(128)S(1)}, f32[128]{0:T(128)}, u32[]{:S(2)}) copy-start(f32[128]{0:T(128)} %param.11) | copy-start | bytes 1540
  6.5 97.0 %all-gather.3.cloned.1.call-start = ((), (), s32[]{:S(2)}) async-start(), calls=%async_computation | async-start | bytes 4325376 | tf_op jit(solution)/shard_map/all_gather | solution.py:141
  10.5 3.2 collective-permute-start
  14.4 181.5 %all-gather.5.cloned.1.call-start = ((), (), s32[]{:S(2)}) async-start(), calls=%async_computation.1 | async-start | bytes 4325376 | tf_op jit(solution)/shard_map/all_gather | solution.py:142
Sparse Core Ops, SparseCore 0:
  14.6 88.9 all-gather.2
  106.6 89.3 all-gather.4
where the time goes:
time: 371 us; the launch traced here: 369 us
  waiting for transfers between devices  173 us (47%)
  matrix products  69.1 us (19%)
  loops' own time  65.2 us (18%)
  local copies, waits for them, and re-layouts  35.7 us (10%)
  between operations  13.6 us (4%)
  other arithmetic  10.7 us (3%)
    all_gather x1, waiting for transfers between devices, per_device(): lax.all_gather(value_rows, 'ctx', axis=0, tiled=True)  86.1 us
    all_gather x1, waiting for transfers between devices, per_device(): lax.all_gather(key_rows, 'ctx', axis=0, tiled=True)  84.9 us
    another operation x1, loops' own time, attend_span(): lax.scan(one_block, running, (key_parts, value_parts, jnp.arange(block_co...  64.2 us
    dot_general x17, matrix products, compute(): jnp.einsum('rhk,kd->rhd', weights.astype(jnp.bfloat16), value_block, pref...  36.5 us
    dot_general x17, matrix products, compute(): jnp.einsum('rhd,kd->rhk', query_part, key_block, preferred_element_type=j...  32.6 us
    dynamic_slice x32, local copies, waits for them, and re-layouts, attend_span(): lax.scan(one_block, running, (key_parts, value_parts, jnp.arange(block_co...  18.8 us
    unnamed x8, local copies, waits for them, and re-layouts  16.2 us
  transfers between devices with their start and end apart: 3, of which 3 were waited for; matrix products, arithmetic and copies ran while one was open for 3% of the time, Pallas kernels for 0%

commit v1 on v0

v1 whole, which is shorter than its diff:
```python
import functools

import jax
import jax.numpy as jnp
import numpy as np
from jax import lax
from jax.experimental import pallas as pl
from jax.experimental.pallas import tpu as pltpu
from jax.sharding import PartitionSpec as P

HD = 128
UNIT = 256
SHARD = 512
UNITS = 2
LOCAL_HEADS = 4
ROWS = LOCAL_HEADS * UNIT
X_SIZE = 4
Z_SIZE = 8
NORM_EPS = 1e-06
ROPE_BASE = 1000000.0

OWN = 0
ORDER = [
    (0, 0),
    (1, 0),
    (2, 0),
    (1, 1),
    (1, 3),
    (3, 0),
    (1, 2),
    (4, 0),
    (2, 1),
    (2, 3),
    (2, 2),
    (3, 1),
    (3, 3),
    (3, 2),
    (None, 1),
    (None, 3),
    (None, 2),
]
SLOT = {place: index for index, place in enumerate(ORDER)}
SLOTS = len(ORDER)


def rope_tables():
    frequency = ROPE_BASE ** (-np.arange(HD // 2, dtype=np.float64) * 2.0 / HD)
    sign = np.concatenate([-np.ones(HD // 2), np.ones(HD // 2)])

    def table(positions):
        angle = positions[:, None].astype(np.float64) * np.concatenate([frequency, frequency])
        return np.concatenate([np.cos(angle), np.sin(angle) * sign], axis=1).astype(np.float32)

    return table(np.arange(UNIT)), table(np.arange(64) * UNIT)


def attention_kernel(
    query_hbm,
    key_value_hbm,
    row_table_hbm,
    query_gain_ref,
    key_gain_ref,
    offsets_ref,
    base_table_ref,
    out_ref,
    query_raw,
    row_table,
    queries,
    blocks,
    totals,
    first_units,
    local_sem,
    send_sem,
    recv_sem,
    half_sem,
    pair_send_sem,
    pair_recv_sem,
):
    ctx = lax.axis_index("ctx")
    head = lax.axis_index("head")
    z, x = ctx // X_SIZE, ctx % X_SIZE
    core = head % 2

    def place(z_to, x_to):
        return (((z_to + Z_SIZE) % Z_SIZE) * X_SIZE + (x_to + X_SIZE) % X_SIZE, head)

    z_next, z_last = place(z + 1, x), place(z - 1, x)
    x_next, x_last, x_across = place(z, x + 1), place(z, x - 1), place(z, x + 2)
    partner = (ctx, head + 1 - 2 * core)

    barrier = pltpu.get_barrier_semaphore()
    for other in (partner, x_next, x_last, z_next, z_last, x_across):
        pl.semaphore_signal(barrier, inc=1, device_id=other, device_id_type=pl.DeviceIdType.MESH)

    own_rows = pl.ds(0, SHARD)
    fetch_own = pltpu.make_async_copy(key_value_hbm, blocks.at[core, own_rows], local_sem.at[0])
    fetch_own.start()
    fetch_table = pltpu.make_async_copy(row_table_hbm, row_table, local_sem.at[1])
    fetch_table.start()
    fetch_query = pltpu.make_async_copy(query_hbm, query_raw, local_sem.at[2])
    fetch_query.start()

    doc_units = []
    for unit in range(UNITS):
        first = (ctx * UNITS + unit) * UNIT
        start = 0
        for entry in range(offsets_ref.shape[0]):
            offset = offsets_ref[entry]
            start = jnp.maximum(start, jnp.where(offset <= first, offset, 0))
        doc_units.append(start // UNIT)

    for index, (row, step) in enumerate(ORDER):
        if row is None:
            shard = jnp.where(x >= step, ctx - step, ctx - 4 * X_SIZE - step + X_SIZE)
        else:
            shard = ctx - row * X_SIZE - step + jnp.where(x >= step, 0, X_SIZE)
        first_units[index] = shard * UNITS

    fetch_table.wait()

    def unit_tables(unit):
        behind = ctx * UNITS + unit - doc_units[unit]
        base = base_table_ref[pl.ds(behind, 1), :]
        base_cos, base_sin = base[:, :HD], base[:, HD:]
        row_cos, row_sin = row_table[:, :HD], row_table[:, HD:]
        cosines = base_cos * row_cos - base_sin * row_sin
        sines = base_sin * row_cos + base_cos * row_sin
        return cosines, sines

    tables = [unit_tables(unit) for unit in range(UNITS)]

    def with_gain(unit, gain_ref):
        gain = gain_ref[...].reshape(1, HD)
        cosines, sines = tables[unit]
        return cosines * gain, sines * pltpu.roll(gain, HD // 2, 1)

    def norm_rotate(rows, gained, scale):
        wide = rows.astype(jnp.float32)
        mean_square = jnp.mean(wide * wide, axis=1, keepdims=True)
        factor = lax.rsqrt(mean_square + NORM_EPS)
        if scale is not None:
            factor = factor * scale
        turned = wide * gained[0] + pltpu.roll(wide, HD // 2, 1) * gained[1]
        return (turned * factor).astype(jnp.bfloat16)

    fetch_own.wait()

    @pl.when(core == 0)
    def _():
        for unit in range(UNITS):
            rows = slice(unit * UNIT, (unit + 1) * UNIT)
            blocks[0, rows, :] = norm_rotate(
                blocks[0, rows, :], with_gain(unit, key_gain_ref), None
            )

    pl.semaphore_wait(barrier, 6)

    def rows_of(slot, half=None):
        if half is None:
            return pl.ds(slot * SHARD, SHARD)
        return pl.ds(slot * SHARD + half * UNIT, UNIT)

    send_count = [0]
    sends = []

    def to_chip(source, target, device, sem, half=None):
        arrival = recv_sem.at[target] if half is None or half == 0 else half_sem.at[target]
        return pltpu.make_async_remote_copy(
            src_ref=blocks.at[core, rows_of(source, half)],
            dst_ref=blocks.at[core, rows_of(target, half)],
            send_sem=send_sem.at[sem],
            recv_sem=arrival,
            device_id=device,
            device_id_type=pl.DeviceIdType.MESH,
        )

    def to_partner(slot):
        return pltpu.make_async_remote_copy(
            src_ref=blocks.at[core, rows_of(slot)],
            dst_ref=blocks.at[core, rows_of(slot)],
            send_sem=pair_send_sem.at[slot],
            recv_sem=pair_recv_sem.at[slot],
            device_id=partner,
            device_id_type=pl.DeviceIdType.MESH,
        )

    def from_partner(slot):
        return pltpu.make_async_remote_copy(
            src_ref=blocks.at[1 - core, rows_of(slot)],
            dst_ref=blocks.at[1 - core, rows_of(slot)],
            send_sem=pair_send_sem.at[slot],
            recv_sem=pair_recv_sem.at[slot],
            device_id=partner,
            device_id_type=pl.DeviceIdType.MESH,
        )

    def send(source, target, device, half=None):
        sem = send_count[0]
        send_count[0] += 1
        to_chip(source, target, device, sem, half).start()
        sends.append((source, target, device, sem, half))

    ahead = {1: x_next, 2: x_across, 3: x_last}
    corner = {}
    for step in (1, 3, 2):
        sem = send_count[0]
        send_count[0] += 1
        corner[step] = sem

    def to_corner(source, step):
        return to_chip(source, SLOT[(None, step)], ahead[step], corner[step])

    def arrived(slot):
        row, step = ORDER[slot]
        if row is not None and step == 2:
            for half in range(2):
                to_chip(slot, slot, x_next, 0, half).wait_recv()
        else:
            to_chip(slot, slot, x_next, 0).wait_recv()
        if row is not None:
            if step == 0:
                if row < 4:
                    send(slot, SLOT[(row + 1, 0)], z_next)
                    send(slot, SLOT[(row, 1)], x_next)
                    send(slot, SLOT[(row, 3)], x_last)
                else:
                    for corner_step in (1, 3, 2):

                        @pl.when(x + corner_step >= X_SIZE)
                        def _():
                            to_corner(SLOT[(4, 0)], corner_step).start()

            if step == 1:
                send(slot, SLOT[(row, 2)], x_next, half=0)
            if step == 3:
                send(slot, SLOT[(row, 2)], x_last, half=1)
        to_partner(slot).start()

    send(OWN, SLOT[(1, 0)], z_next)
    for corner_step in (1, 3, 2):

        @pl.when(x + corner_step < X_SIZE)
        def _():
            to_corner(OWN, corner_step).start()

    to_partner(OWN).start()

    fetch_query.wait()
    for unit in range(UNITS):
        gained = with_gain(unit, query_gain_ref)
        for local in range(LOCAL_HEADS):
            rows = query_raw[
                unit * UNIT : (unit + 1) * UNIT, local * HD : (local + 1) * HD
            ]
            queries[unit, local * UNIT : (local + 1) * UNIT, :] = norm_rotate(
                rows, gained, HD**-0.5
            )

    def scores(unit, part, part_rows, keys):
        return lax.dot_general(
            queries[unit, part * part_rows : (part + 1) * part_rows, :],
            keys,
            (((1,), (1,)), ((), ())),
            preferred_element_type=jnp.float32,
        )

    def masked_values(values, allowed):
        zero = jnp.zeros_like(values)
        return jnp.concatenate(
            [jnp.where(allowed, values, zero), jnp.where(allowed, zero + 1, zero)], axis=1
        )

    from_partner(OWN).wait_recv()
    own_first = ctx * UNITS
    for unit in range(UNITS):
        count = (unit + 1) * UNIT
        keys = blocks[0, :count, :]
        unit_of_key = own_first + lax.broadcasted_iota(jnp.int32, (count, HD), 0) // UNIT
        values = masked_values(blocks[1, :count, :], unit_of_key >= doc_units[unit])
        part_rows = 512
        for part in range(ROWS // part_rows):
            shape = (part_rows, count)
            position = lax.broadcasted_iota(jnp.int32, shape, 0) % UNIT + unit * UNIT
            causal = lax.broadcasted_iota(jnp.int32, shape, 1) <= position
            weights = jnp.where(
                causal, jnp.exp(scores(unit, part, part_rows, keys)), 0.0
            ).astype(jnp.bfloat16)
            totals[unit, part * part_rows : (part + 1) * part_rows, :] = jnp.dot(
                weights, values, preferred_element_type=jnp.float32
            )

    def attend(slot, width):
        count = width * SHARD
        at = pl.ds(pl.multiple_of(slot * SHARD, SHARD), count)
        keys = blocks[0, at, :]
        values = blocks[1, at, :]
        row = lax.broadcasted_iota(jnp.int32, (SHARD, HD), 0) // UNIT
        key_unit = jnp.concatenate(
            [row + first_units[slot + place] for place in range(width)], axis=0
        )
        masked = [masked_values(values, key_unit >= doc_units[unit]) for unit in range(UNITS)]
        part_rows = 512
        parts = [(unit, part) for unit in range(UNITS) for part in range(ROWS // part_rows)]
        held = scores(*parts[0], part_rows, keys)
        for index, (unit, part) in enumerate(parts):
            later = None
            if index + 1 < len(parts):
                later = scores(*parts[index + 1], part_rows, keys)
            weights = jnp.exp(held).astype(jnp.bfloat16)
            totals[unit, part * part_rows : (part + 1) * part_rows, :] += jnp.dot(
                weights, masked[unit], preferred_element_type=jnp.float32
            )
            held = later

    def wait_partner(slot, width):
        for place in range(width):
            from_partner(slot + place).wait_recv()

    single_events = {1: [(1, 0)], 2: [(2, 0)]}
    pair_events = {
        0: [(1, 1), (1, 3)],
        1: [(3, 0), (1, 2)],
        2: [(4, 0), (2, 1), (2, 3)],
        3: [(2, 2)],
        4: [(3, 1), (3, 3)],
        5: [(3, 2), (None, 1)],
        6: [(None, 3), (None, 2)],
    }

    def single(slot, carry):
        for index, places in single_events.items():

            @pl.when(slot == index)
            def _():
                for where in places:
                    arrived(SLOT[where])

        wait_partner(slot, 1)
        attend(slot, 1)
        return carry

    lax.fori_loop(1, 3, single, 0)

    def pair(step, carry):
        for index, places in pair_events.items():

            @pl.when(step == index)
            def _():
                for where in places:
                    arrived(SLOT[where])

        slot = 3 + 2 * step
        wait_partner(slot, 2)
        attend(slot, 2)
        return carry

    lax.fori_loop(0, 7, pair, 0)

    for unit in range(UNITS):
        for local in range(LOCAL_HEADS):
            rows = slice(local * UNIT, (local + 1) * UNIT)
            out_ref[unit * UNIT : (unit + 1) * UNIT, local * HD : (local + 1) * HD] = (
                totals[unit, rows, :HD] / totals[unit, rows, HD:]
            ).astype(jnp.bfloat16)

    for copy in sends:
        to_chip(*copy).wait_send()
    for step in (1, 3, 2):
        to_corner(OWN, step).wait_send()
    for slot in range(SLOTS):
        to_partner(slot).wait_send()


def per_device(query_proj, key_value, query_gain, key_gain, doc_offsets):
    row_table, base_table = rope_tables()
    any_space = pl.BlockSpec(memory_space=pl.ANY)
    vmem = pl.BlockSpec(memory_space=pltpu.VMEM)
    return pl.pallas_call(
        attention_kernel,
        out_shape=jax.ShapeDtypeStruct((SHARD, LOCAL_HEADS * HD), jnp.bfloat16),
        in_specs=[
            any_space,
            any_space,
            any_space,
            vmem,
            vmem,
            pl.BlockSpec(memory_space=pltpu.SMEM),
            vmem,
        ],
        out_specs=vmem,
        scratch_shapes=[
            pltpu.VMEM((SHARD, LOCAL_HEADS * HD), jnp.bfloat16),
            pltpu.VMEM((UNIT, 2 * HD), jnp.float32),
            pltpu.VMEM((UNITS, ROWS, HD), jnp.bfloat16),
            pltpu.VMEM((2, SLOTS * SHARD, HD), jnp.bfloat16),
            pltpu.VMEM((UNITS, ROWS, 2 * HD), jnp.float32),
            pltpu.SMEM((SLOTS,), jnp.int32),
            pltpu.SemaphoreType.DMA((3,)),
            pltpu.SemaphoreType.DMA((24,)),
            pltpu.SemaphoreType.DMA((SLOTS,)),
            pltpu.SemaphoreType.DMA((SLOTS,)),
            pltpu.SemaphoreType.DMA((SLOTS,)),
            pltpu.SemaphoreType.DMA((SLOTS,)),
        ],
        compiler_params=pltpu.CompilerParams(
            collective_id=0, has_side_effects=True, vmem_limit_bytes=48 * 1024 * 1024
        ),
        cost_estimate=pl.CostEstimate(
            flops=2 * 2 * 2048 * 8448 * HD, bytes_accessed=2 << 20, transcendentals=2048 * 8448
        ),
    )(
        query_proj,
        key_value,
        jnp.asarray(row_table),
        query_gain,
        key_gain,
        doc_offsets,
        jnp.asarray(base_table),
    )


def solution(mesh):
    placed = (P("ctx", "head"), P("ctx", "head"), P(), P(), P())
    return jax.shard_map(
        per_device, mesh=mesh, in_specs=placed, out_specs=P("ctx", "head"), check_vma=False
    )
```

time: 371 us -> 63.9 us (0.17)
  the two profiles are of different devices: /device:TPU:468 before, /device:TPU:1 now
where the time goes in v1:
time: 63.9 us; the launch traced here: 63.6 us
  Pallas kernels  57.1 us (89%)
  local copies, waits for them, and re-layouts  6.49 us (10%)
    pallas_call x1, Pallas kernels, per_device(): pl.pallas_call(attention_kernel, out_shape=jax.ShapeDtypeStruct((SHARD, L...  57.1 us
    unnamed x15, local copies, waits for them, and re-layouts  6.49 us

profile of v1, /device:TPU:1, one launch (start us, length us, event | category | flops | bytes accessed | tf_op | source)
XLA Modules:
  0.0 63.6 jit_solution(15857357677458569101)
XLA Ops:
  0.0 0.0 copy-start
  0.0 1.0 %copy-done = bf16[512,512]{1,0:T(8,128)(2,1)S(1)} copy-done((bf16[512,512]{1,0:T(8,128)(2,1)S(1)}, bf16[512,512]{1,0:T(8,128)(2,1)}, u32[]{:S(2)}) %copy-start) | copy-done | bytes 524312
  1.0 0.0 copy-start.1
  1.0 0.9 %copy-done.1 = bf16[512,128]{1,0:T(8,128)(2,1)S(1)} copy-done((bf16[512,128]{1,0:T(8,128)(2,1)S(1)}, bf16[512,128]{1,0:T(8,128)(2,1)}, u32[]{:S(2)}) %copy-start.1) | copy-done | bytes 131096
  1.9 0.0 copy-start.2
  1.9 0.7 %copy-done.2 = f32[128]{0:T(128)S(1)} copy-done((f32[128]{0:T(128)S(1)}, f32[128]{0:T(128)}, u32[]{:S(2)}) %copy-start.2) | copy-done | bytes 536
  2.6 0.0 copy-start.3
  2.6 0.7 %copy-done.3 = f32[128]{0:T(128)S(1)} copy-done((f32[128]{0:T(128)S(1)}, f32[128]{0:T(128)}, u32[]{:S(2)}) %copy-start.3) | copy-done | bytes 536
  3.3 0.0 copy-start.4
  3.3 0.7 %copy-done.4 = s32[65]{0:T(128)S(1)} copy-done((s32[65]{0:T(128)S(1)}, s32[65]{0:T(128)}, u32[]{:S(2)}) %copy-start.4) | copy-done | bytes 284
  3.9 0.0 copy-start.5
  3.9 0.9 %copy-done.5 = f32[256,256]{1,0:T(8,128)S(1)} copy-done((f32[256,256]{1,0:T(8,128)S(1)}, f32[256,256]{1,0:T(8,128)}, u32[]{:S(2)}) %copy-start.5) | copy-done | bytes 262168
  4.9 0.0 copy-start.6
  4.9 0.8 %copy-done.6 = f32[64,256]{1,0:T(8,128)S(1)} copy-done((f32[64,256]{1,0:T(8,128)S(1)}, f32[64,256]{1,0:T(8,128)}, u32[]{:S(2)}) %copy-start.6) | copy-done | bytes 65560
  5.7 57.1 %shard_map.73 = bf16[512,512]{1,0:T(8,128)(2,1)S(1)} custom-call(bf16[512,512]{1,0:T(8,128)(2,1)S(1)} %copy-done, bf16[512,128]{1,0:T(8,128)(2,1)S(1)} %copy-done.1, f32[256,256]{1,0:T(8,128)S(1)} %copy-done.5, f32[128]{0:T(128)S(1)} %copy-done.2, f32[128]{0:T(128)S(1)} %copy-done.3, s32[65]{0:T(128)S(1)} %copy-done.4, f32[64,256]{1,0:T(8,128)S(1)} %copy-done.6), custom_call_target="tpu_custom_call" | custom-call | flops 8858370048 | bytes 2097152 | tf_op jit(solution)/shard_map/pallas_call | solution.py:378
  62.8 0.8 %copy.9 = bf16[512,512]{1,0:T(8,128)(2,1)} copy(bf16[512,512]{1,0:T(8,128)(2,1)S(1)} %shard_map.73) | data formatting | bytes 1048576
Async XLA Ops:
  0.0 1.0 %copy-start = (bf16[512,512]{1,0:T(8,128)(2,1)S(1)}, bf16[512,512]{1,0:T(8,128)(2,1)}, u32[]{:S(2)}) copy-start(bf16[512,512]{1,0:T(8,128)(2,1)} %query_hbm.1) | copy-start | bytes 1572868
  1.0 0.9 %copy-start.1 = (bf16[512,128]{1,0:T(8,128)(2,1)S(1)}, bf16[512,128]{1,0:T(8,128)(2,1)}, u32[]{:S(2)}) copy-start(bf16[512,128]{1,0:T(8,128)(2,1)} %key_value_hbm.1) | copy-start | bytes 393220
  1.9 0.7 %copy-start.2 = (f32[128]{0:T(128)S(1)}, f32[128]{0:T(128)}, u32[]{:S(2)}) copy-start(f32[128]{0:T(128)} %query_gain_ref.1) | copy-start | bytes 1540
  2.6 0.7 %copy-start.3 = (f32[128]{0:T(128)S(1)}, f32[128]{0:T(128)}, u32[]{:S(2)}) copy-start(f32[128]{0:T(128)} %key_gain_ref.1) | copy-start | bytes 1540
  3.3 0.7 %copy-start.4 = (s32[65]{0:T(128)S(1)}, s32[65]{0:T(128)}, u32[]{:S(2)}) copy-start(s32[65]{0:T(128)} %offsets_ref.1) | copy-start | bytes 784
  3.9 0.9 %copy-start.5 = (f32[256,256]{1,0:T(8,128)S(1)}, f32[256,256]{1,0:T(8,128)}, u32[]{:S(2)}) copy-start(f32[256,256]{1,0:T(8,128)} %constant.4.clone.row_table_hbm) | copy-start | bytes 786436
  4.9 0.8 %copy-start.6 = (f32[64,256]{1,0:T(8,128)S(1)}, f32[64,256]{1,0:T(8,128)}, u32[]{:S(2)}) copy-start(f32[64,256]{1,0:T(8,128)} %constant.5.clone.base_table_ref) | copy-start | bytes 196612

commit v2 on v1

--- a/solution.py
+++ b/solution.py
@@ -28,9 +28,9 @@
     (1, 3),
     (3, 0),
     (1, 2),
-    (4, 0),
     (2, 1),
     (2, 3),
+    (4, 0),
     (2, 2),
     (3, 1),
     (3, 3),
@@ -58,13 +58,17 @@
     query_hbm,
     key_value_hbm,
     row_table_hbm,
+    query_gain_hbm,
+    key_gain_hbm,
+    offsets_hbm,
+    base_table_hbm,
+    out_ref,
+    query_raw,
+    row_table,
     query_gain_ref,
     key_gain_ref,
     offsets_ref,
     base_table_ref,
-    out_ref,
-    query_raw,
-    row_table,
     queries,
     blocks,
     totals,
@@ -89,17 +93,41 @@
     partner = (ctx, head + 1 - 2 * core)
 
     barrier = pltpu.get_barrier_semaphore()
-    for other in (partner, x_next, x_last, z_next, z_last, x_across):
+
+    def greet(other):
         pl.semaphore_signal(barrier, inc=1, device_id=other, device_id_type=pl.DeviceIdType.MESH)
 
+    @pl.when(z > 0)
+    def _():
+        greet(z_last)
+
+    @pl.when(z < Z_SIZE - 1)
+    def _():
+        greet(z_next)
+
+    for other in (x_next, x_last, x_across, partner):
+        greet(other)
+
     own_rows = pl.ds(0, SHARD)
-    fetch_own = pltpu.make_async_copy(key_value_hbm, blocks.at[core, own_rows], local_sem.at[0])
-    fetch_own.start()
-    fetch_table = pltpu.make_async_copy(row_table_hbm, row_table, local_sem.at[1])
-    fetch_table.start()
-    fetch_query = pltpu.make_async_copy(query_hbm, query_raw, local_sem.at[2])
-    fetch_query.start()
-
+    fetches = [
+        pltpu.make_async_copy(source, target, local_sem.at[index])
+        for index, (source, target) in enumerate(
+            (
+                (offsets_hbm, offsets_ref),
+                (base_table_hbm, base_table_ref),
+                (key_gain_hbm, key_gain_ref),
+                (key_value_hbm, blocks.at[core, own_rows]),
+                (row_table_hbm, row_table),
+                (query_gain_hbm, query_gain_ref),
+                (query_hbm, query_raw),
+            )
+        )
+    ]
+    for fetch in fetches:
+        fetch.start()
+    fetch_offsets, fetch_base, fetch_key_gain, fetch_own, fetch_table, fetch_gain, fetch_query = fetches
+
+    fetch_offsets.wait()
     doc_units = []
     for unit in range(UNITS):
         first = (ctx * UNITS + unit) * UNIT
@@ -116,6 +144,8 @@
             shard = ctx - row * X_SIZE - step + jnp.where(x >= step, 0, X_SIZE)
         first_units[index] = shard * UNITS
 
+    fetch_base.wait()
+    fetch_key_gain.wait()
     fetch_table.wait()
 
     def unit_tables(unit):
@@ -153,18 +183,29 @@
                 blocks[0, rows, :], with_gain(unit, key_gain_ref), None
             )
 
-    pl.semaphore_wait(barrier, 6)
-
     def rows_of(slot, half=None):
         if half is None:
             return pl.ds(slot * SHARD, SHARD)
         return pl.ds(slot * SHARD + half * UNIT, UNIT)
 
-    send_count = [0]
-    sends = []
+    def holds(slot):
+        row, step = ORDER[slot]
+        if row is None:
+            return jnp.logical_or(x >= step, z >= 4)
+        return z >= row
+
+    for slot in range(1, SLOTS):
+
+        @pl.when(jnp.logical_not(holds(slot)))
+        def _():
+            blocks[0, rows_of(slot), :] = jnp.zeros((SHARD, HD), jnp.bfloat16)
+
+    pl.semaphore_wait(
+        barrier, 4 + jnp.where(z > 0, 1, 0) + jnp.where(z < Z_SIZE - 1, 1, 0)
+    )
 
     def to_chip(source, target, device, sem, half=None):
-        arrival = recv_sem.at[target] if half is None or half == 0 else half_sem.at[target]
+        arrival = half_sem.at[target] if half == 1 else recv_sem.at[target]
         return pltpu.make_async_remote_copy(
             src_ref=blocks.at[core, rows_of(source, half)],
             dst_ref=blocks.at[core, rows_of(target, half)],
@@ -194,59 +235,68 @@
             device_id_type=pl.DeviceIdType.MESH,
         )
 
-    def send(source, target, device, half=None):
-        sem = send_count[0]
-        send_count[0] += 1
-        to_chip(source, target, device, sem, half).start()
-        sends.append((source, target, device, sem, half))
+    sends = []
+
+    def plan(source, target, device, half, condition):
+        sends.append((source, target, device, half, condition))
 
     ahead = {1: x_next, 2: x_across, 3: x_last}
-    corner = {}
+    below = z < Z_SIZE - 1
+    for half in range(2):
+        plan(OWN, SLOT[(1, 0)], z_next, half, below)
     for step in (1, 3, 2):
-        sem = send_count[0]
-        send_count[0] += 1
-        corner[step] = sem
-
-    def to_corner(source, step):
-        return to_chip(source, SLOT[(None, step)], ahead[step], corner[step])
-
-    def arrived(slot):
-        row, step = ORDER[slot]
-        if row is not None and step == 2:
-            for half in range(2):
-                to_chip(slot, slot, x_next, 0, half).wait_recv()
+        plan(OWN, SLOT[(None, step)], ahead[step], None, x + step < X_SIZE)
+    for row in (1, 2, 3):
+        have = z >= row
+        slot = SLOT[(row, 0)]
+        for half in range(2):
+            plan(slot, SLOT[(row + 1, 0)], z_next, half, jnp.logical_and(have, below))
+            plan(slot, SLOT[(row, 1)], x_next, half, have)
+            plan(slot, SLOT[(row, 3)], x_last, half, have)
+        plan(SLOT[(row, 1)], SLOT[(row, 2)], x_next, 0, have)
+        plan(SLOT[(row, 3)], SLOT[(row, 2)], x_last, 1, have)
+    for step in (1, 3, 2):
+        condition = jnp.logical_and(x + step >= X_SIZE, z >= 4)
+        plan(SLOT[(4, 0)], SLOT[(None, step)], ahead[step], None, condition)
+
+    def send_from(slot, halves):
+        for sem, (source, target, device, half, condition) in enumerate(sends):
+            if source == slot and half in halves:
+
+                @pl.when(condition)
+                def _():
+                    to_chip(source, target, device, sem, half).start()
+
+    def arrived(place, half=None):
+        slot = SLOT[place]
+        if place[0] is None:
+            halves = (None,)
+        elif half is None:
+            halves = (0, 1)
         else:
-            to_chip(slot, slot, x_next, 0).wait_recv()
-        if row is not None:
-            if step == 0:
-                if row < 4:
-                    send(slot, SLOT[(row + 1, 0)], z_next)
-                    send(slot, SLOT[(row, 1)], x_next)
-                    send(slot, SLOT[(row, 3)], x_last)
-                else:
-                    for corner_step in (1, 3, 2):
-
-                        @pl.when(x + corner_step >= X_SIZE)
-                        def _():
-                            to_corner(SLOT[(4, 0)], corner_step).start()
-
-            if step == 1:
-                send(slot, SLOT[(row, 2)], x_next, half=0)
-            if step == 3:
-                send(slot, SLOT[(row, 2)], x_last, half=1)
-        to_partner(slot).start()
-
-    send(OWN, SLOT[(1, 0)], z_next)
-    for corner_step in (1, 3, 2):
-
-        @pl.when(x + corner_step < X_SIZE)
+            halves = (half,)
+
+        @pl.when(holds(slot))
         def _():
-            to_corner(OWN, corner_step).start()
+            for part in halves:
+                to_chip(slot, slot, x_next, 0, part).wait_recv()
+            if halves[-1] != 0:
+                to_partner(slot).start()
+
+        send_from(slot, halves + (None,) if halves[-1] == 1 else halves)
+
+    def wait_partner(slot):
+        @pl.when(holds(slot))
+        def _():
+            from_partner(slot).wait_recv()
 
     to_partner(OWN).start()
-
+    send_from(OWN, (None, 0, 1))
+
+    fetch_gain.wait()
     fetch_query.wait()
-    for unit in range(UNITS):
+
+    def prepare_queries(unit):
         gained = with_gain(unit, query_gain_ref)
         for local in range(LOCAL_HEADS):
             rows = query_raw[
@@ -270,9 +320,9 @@
             [jnp.where(allowed, values, zero), jnp.where(allowed, zero + 1, zero)], axis=1
         )
 
-    from_partner(OWN).wait_recv()
     own_first = ctx * UNITS
-    for unit in range(UNITS):
+
+    def attend_own(unit):
         count = (unit + 1) * UNIT
         keys = blocks[0, :count, :]
         unit_of_key = own_first + lax.broadcasted_iota(jnp.int32, (count, HD), 0) // UNIT
@@ -289,6 +339,14 @@
                 weights, values, preferred_element_type=jnp.float32
             )
 
+    prepare_queries(0)
+    prepare_queries(1)
+    from_partner(OWN).wait_recv()
+    attend_own(0)
+    arrived((1, 0), 0)
+    attend_own(1)
+    arrived((1, 0), 1)
+
     def attend(slot, width):
         count = width * SHARD
         at = pl.ds(pl.multiple_of(slot * SHARD, SHARD), count)
@@ -312,49 +370,45 @@
             )
             held = later
 
-    def wait_partner(slot, width):
-        for place in range(width):
-            from_partner(slot + place).wait_recv()
-
-    single_events = {1: [(1, 0)], 2: [(2, 0)]}
+    single_events = {
+        1: [((2, 0), 0), ((2, 0), 1)],
+        2: [((1, 1), 0), ((1, 3), 0), ((1, 1), 1), ((1, 3), 1)],
+        3: [((3, 0), 0), ((3, 0), 1)],
+        4: [((1, 2),)],
+    }
     pair_events = {
-        0: [(1, 1), (1, 3)],
-        1: [(3, 0), (1, 2)],
-        2: [(4, 0), (2, 1), (2, 3)],
-        3: [(2, 2)],
-        4: [(3, 1), (3, 3)],
-        5: [(3, 2), (None, 1)],
-        6: [(None, 3), (None, 2)],
+        0: [((2, 1),), ((2, 3),), ((4, 0),)],
+        1: [((2, 2),)],
+        2: [((3, 1),), ((3, 3),)],
+        3: [((3, 2),), ((None, 1),)],
+        4: [((None, 3),), ((None, 2),)],
+        5: [],
     }
-
-    def single(slot, carry):
-        for index, places in single_events.items():
-
-            @pl.when(slot == index)
-            def _():
-                for where in places:
-                    arrived(SLOT[where])
-
-        wait_partner(slot, 1)
-        attend(slot, 1)
-        return carry
-
-    lax.fori_loop(1, 3, single, 0)
-
-    def pair(step, carry):
-        for index, places in pair_events.items():
+    singles = len(single_events)
+
+    def take(step, events, first, width):
+        for index, arrivals in events.items():
 
             @pl.when(step == index)
             def _():
-                for where in places:
-                    arrived(SLOT[where])
-
-        slot = 3 + 2 * step
-        wait_partner(slot, 2)
-        attend(slot, 2)
+                for arrival in arrivals:
+                    arrived(*arrival)
+                for place in range(width):
+                    wait_partner(first + width * index + place)
+
+    def single(step, carry):
+        take(step, single_events, 0, 1)
+        attend(step, 1)
         return carry
 
-    lax.fori_loop(0, 7, pair, 0)
+    lax.fori_loop(1, 1 + singles, single, 0)
+
+    def pair(step, carry):
+        take(step, pair_events, 1 + singles, 2)
+        attend(1 + singles + 2 * step, 2)
+        return carry
+
+    lax.fori_loop(0, len(pair_events), pair, 0)
 
     for unit in range(UNITS):
         for local in range(LOCAL_HEADS):
@@ -363,47 +417,46 @@
                 totals[unit, rows, :HD] / totals[unit, rows, HD:]
             ).astype(jnp.bfloat16)
 
-    for copy in sends:
-        to_chip(*copy).wait_send()
-    for step in (1, 3, 2):
-        to_corner(OWN, step).wait_send()
+    for sem, (source, target, device, half, condition) in enumerate(sends):
+
+        @pl.when(condition)
+        def _():
+            to_chip(source, target, device, sem, half).wait_send()
+
     for slot in range(SLOTS):
-        to_partner(slot).wait_send()
+
+        @pl.when(holds(slot))
+        def _():
+            to_partner(slot).wait_send()
 
 
 def per_device(query_proj, key_value, query_gain, key_gain, doc_offsets):
     row_table, base_table = rope_tables()
-    any_space = pl.BlockSpec(memory_space=pl.ANY)
-    vmem = pl.BlockSpec(memory_space=pltpu.VMEM)
     return pl.pallas_call(
         attention_kernel,
         out_shape=jax.ShapeDtypeStruct((SHARD, LOCAL_HEADS * HD), jnp.bfloat16),
-        in_specs=[
-            any_space,
-            any_space,
-            any_space,
-            vmem,
-            vmem,
-            pl.BlockSpec(memory_space=pltpu.SMEM),
-            vmem,
-        ],
-        out_specs=vmem,
+        in_specs=[pl.BlockSpec(memory_space=pltpu.HBM)] * 7,
+        out_specs=pl.BlockSpec(memory_space=pltpu.VMEM),
         scratch_shapes=[
             pltpu.VMEM((SHARD, LOCAL_HEADS * HD), jnp.bfloat16),
             pltpu.VMEM((UNIT, 2 * HD), jnp.float32),
+            pltpu.VMEM((HD,), jnp.float32),
+            pltpu.VMEM((HD,), jnp.float32),
+            pltpu.SMEM(doc_offsets.shape, jnp.int32),
+            pltpu.VMEM((64, 2 * HD), jnp.float32),
             pltpu.VMEM((UNITS, ROWS, HD), jnp.bfloat16),
             pltpu.VMEM((2, SLOTS * SHARD, HD), jnp.bfloat16),
             pltpu.VMEM((UNITS, ROWS, 2 * HD), jnp.float32),
             pltpu.SMEM((SLOTS,), jnp.int32),
-            pltpu.SemaphoreType.DMA((3,)),
-            pltpu.SemaphoreType.DMA((24,)),
+            pltpu.SemaphoreType.DMA((7,)),
+            pltpu.SemaphoreType.DMA((40,)),
             pltpu.SemaphoreType.DMA((SLOTS,)),
             pltpu.SemaphoreType.DMA((SLOTS,)),
             pltpu.SemaphoreType.DMA((SLOTS,)),
             pltpu.SemaphoreType.DMA((SLOTS,)),
         ],
         compiler_params=pltpu.CompilerParams(
-            collective_id=0, has_side_effects=True, vmem_limit_bytes=48 * 1024 * 1024
+            collective_id=0, has_side_effects=True, vmem_limit_bytes=64 * 1024 * 1024
         ),
         cost_estimate=pl.CostEstimate(
             flops=2 * 2 * 2048 * 8448 * HD, bytes_accessed=2 << 20, transcendentals=2048 * 8448

time: 63.9 us -> 42.6 us (0.67)
  the two profiles are of different devices: /device:TPU:1 before, /device:TPU:504 now
where the time goes in v2:
time: 42.6 us; the launch traced here: 42.2 us
  Pallas kernels  40.3 us (95%)
  local copies, waits for them, and re-layouts  1.87 us (4%)
    pallas_call x1, Pallas kernels, per_device(): pl.pallas_call(attention_kernel, out_shape=jax.ShapeDtypeStruct((SHARD, L...  40.3 us
    unnamed x1, local copies, waits for them, and re-layouts  1.87 us

profile of v2, /device:TPU:504, one launch (start us, length us, event | category | flops | bytes accessed | tf_op | source)
XLA Modules:
  0.0 42.2 jit_solution(13285764703052470083)
XLA Ops:
  0.0 40.3 %shard_map.73 = bf16[512,512]{1,0:T(8,128)(2,1)} custom-call(bf16[512,512]{1,0:T(8,128)(2,1)} %query_hbm.1, bf16[512,128]{1,0:T(8,128)(2,1)} %key_value_hbm.1, f32[256,256]{1,0:T(8,128)} %constant.4.clone.row_table_hbm, f32[128]{0:T(128)} %query_gain_hbm.1, f32[128]{0:T(128)} %key_gain_hbm.1, s32[65]{0:T(128)} %offsets_hbm.1, ...), custom_call_target="tpu_custom_call" | custom-call | flops 8858370048 | bytes 2097152 | tf_op jit(solution)/shard_map/pallas_call | solution.py:435
  40.3 1.9 %copy.9 = bf16[512,512]{1,0:T(8,128)(2,1)} copy(bf16[512,512]{1,0:T(8,128)(2,1)} %shard_map.73) | data formatting | bytes 1048576

commit v3 on v2

--- a/solution.py
+++ b/solution.py
@@ -24,21 +24,23 @@
     (0, 0),
     (1, 0),
     (2, 0),
+    (3, 0),
     (1, 1),
     (1, 3),
-    (3, 0),
+    (4, 0),
+    (2, 3),
+    (2, 1),
     (1, 2),
-    (2, 1),
-    (2, 3),
-    (4, 0),
+    (3, 3),
+    (3, 1),
     (2, 2),
-    (3, 1),
-    (3, 3),
+    (None, 1),
     (3, 2),
-    (None, 1),
     (None, 3),
     (None, 2),
 ]
+EARLY = [((1, 0), 0), ((1, 0), 1), ((2, 0), 0), ((2, 0), 1)]
+ALONG_Z = ((3, 2), (2, 2), (3, 1))
 SLOT = {place: index for index, place in enumerate(ORDER)}
 SLOTS = len(ORDER)
 
@@ -173,16 +175,6 @@
         turned = wide * gained[0] + pltpu.roll(wide, HD // 2, 1) * gained[1]
         return (turned * factor).astype(jnp.bfloat16)
 
-    fetch_own.wait()
-
-    @pl.when(core == 0)
-    def _():
-        for unit in range(UNITS):
-            rows = slice(unit * UNIT, (unit + 1) * UNIT)
-            blocks[0, rows, :] = norm_rotate(
-                blocks[0, rows, :], with_gain(unit, key_gain_ref), None
-            )
-
     def rows_of(slot, half=None):
         if half is None:
             return pl.ds(slot * SHARD, SHARD)
@@ -193,16 +185,6 @@
         if row is None:
             return jnp.logical_or(x >= step, z >= 4)
         return z >= row
-
-    for slot in range(1, SLOTS):
-
-        @pl.when(jnp.logical_not(holds(slot)))
-        def _():
-            blocks[0, rows_of(slot), :] = jnp.zeros((SHARD, HD), jnp.bfloat16)
-
-    pl.semaphore_wait(
-        barrier, 4 + jnp.where(z > 0, 1, 0) + jnp.where(z < Z_SIZE - 1, 1, 0)
-    )
 
     def to_chip(source, target, device, sem, half=None):
         arrival = half_sem.at[target] if half == 1 else recv_sem.at[target]
@@ -251,10 +233,17 @@
         slot = SLOT[(row, 0)]
         for half in range(2):
             plan(slot, SLOT[(row + 1, 0)], z_next, half, jnp.logical_and(have, below))
-            plan(slot, SLOT[(row, 1)], x_next, half, have)
-            plan(slot, SLOT[(row, 3)], x_last, half, have)
-        plan(SLOT[(row, 1)], SLOT[(row, 2)], x_next, 0, have)
-        plan(SLOT[(row, 3)], SLOT[(row, 2)], x_last, 1, have)
+            if (row, 1) not in ALONG_Z:
+                plan(slot, SLOT[(row, 1)], x_next, half, have)
+            if (row, 3) not in ALONG_Z:
+                plan(slot, SLOT[(row, 3)], x_last, half, have)
+            for step in (1, 2, 3):
+                if (row + 1, step) in ALONG_Z:
+                    target = SLOT[(row + 1, step)]
+                    plan(SLOT[(row, step)], target, z_next, half, jnp.logical_and(have, below))
+        if (row, 2) not in ALONG_Z:
+            plan(SLOT[(row, 1)], SLOT[(row, 2)], x_next, 0, have)
+            plan(SLOT[(row, 3)], SLOT[(row, 2)], x_last, 1, have)
     for step in (1, 3, 2):
         condition = jnp.logical_and(x + step >= X_SIZE, z >= 4)
         plan(SLOT[(4, 0)], SLOT[(None, step)], ahead[step], None, condition)
@@ -290,8 +279,32 @@
         def _():
             from_partner(slot).wait_recv()
 
+    fetch_own.wait()
+
+    def prepare_keys(unit):
+        @pl.when(core == 0)
+        def _():
+            rows = slice(unit * UNIT, (unit + 1) * UNIT)
+            blocks[0, rows, :] = norm_rotate(
+                blocks[0, rows, :], with_gain(unit, key_gain_ref), None
+            )
+
+    prepare_keys(0)
+    for slot in range(1, SLOTS):
+
+        @pl.when(jnp.logical_not(holds(slot)))
+        def _():
+            blocks[0, rows_of(slot), :] = jnp.zeros((SHARD, HD), jnp.bfloat16)
+
+    pl.semaphore_wait(
+        barrier, 4 + jnp.where(z > 0, 1, 0) + jnp.where(z < Z_SIZE - 1, 1, 0)
+    )
+
+    send_from(OWN, (0,))
+    prepare_keys(1)
+    send_from(OWN, (1,))
     to_partner(OWN).start()
-    send_from(OWN, (None, 0, 1))
+    send_from(OWN, (None,))
 
     fetch_gain.wait()
     fetch_query.wait()
@@ -322,30 +335,47 @@
 
     own_first = ctx * UNITS
 
-    def attend_own(unit):
-        count = (unit + 1) * UNIT
-        keys = blocks[0, :count, :]
-        unit_of_key = own_first + lax.broadcasted_iota(jnp.int32, (count, HD), 0) // UNIT
-        values = masked_values(blocks[1, :count, :], unit_of_key >= doc_units[unit])
-        part_rows = 512
-        for part in range(ROWS // part_rows):
-            shape = (part_rows, count)
-            position = lax.broadcasted_iota(jnp.int32, shape, 0) % UNIT + unit * UNIT
-            causal = lax.broadcasted_iota(jnp.int32, shape, 1) <= position
-            weights = jnp.where(
-                causal, jnp.exp(scores(unit, part, part_rows, keys)), 0.0
-            ).astype(jnp.bfloat16)
-            totals[unit, part * part_rows : (part + 1) * part_rows, :] = jnp.dot(
-                weights, values, preferred_element_type=jnp.float32
+    def attend_own():
+        keys = blocks[0, : UNITS * UNIT, :]
+        row = lax.broadcasted_iota(jnp.int32, (SHARD, HD), 0) // UNIT
+        unit_of_key = own_first + row
+        shape = (UNIT, UNIT)
+        causal = lax.broadcasted_iota(jnp.int32, shape, 1) <= lax.broadcasted_iota(
+            jnp.int32, shape, 0
+        )
+        values = [
+            masked_values(blocks[1, :SHARD, :], unit_of_key >= doc_units[unit])
+            for unit in range(UNITS)
+        ]
+        parts = [(unit, part) for unit in range(UNITS) for part in range(LOCAL_HEADS)]
+
+        def part_scores(unit, part):
+            return scores(unit, part, UNIT, keys[: (unit + 1) * UNIT])
+
+        held = part_scores(*parts[0])
+        for index, (unit, part) in enumerate(parts):
+            later = None
+            if index + 1 < len(parts):
+                later = part_scores(*parts[index + 1])
+            weights = jnp.exp(held)
+            corner_weights = jnp.where(causal, weights[:, unit * UNIT :], 0.0)
+            if unit:
+                weights = jnp.concatenate([weights[:, : unit * UNIT], corner_weights], axis=1)
+            else:
+                weights = corner_weights
+            totals[unit, part * UNIT : (part + 1) * UNIT, :] = jnp.dot(
+                weights.astype(jnp.bfloat16),
+                values[unit][: (unit + 1) * UNIT],
+                preferred_element_type=jnp.float32,
             )
+            held = later
 
     prepare_queries(0)
     prepare_queries(1)
     from_partner(OWN).wait_recv()
-    attend_own(0)
-    arrived((1, 0), 0)
-    attend_own(1)
-    arrived((1, 0), 1)
+    for arrival in EARLY:
+        arrived(*arrival)
+    attend_own()
 
     def attend(slot, width):
         count = width * SHARD
@@ -371,18 +401,20 @@
             held = later
 
     single_events = {
-        1: [((2, 0), 0), ((2, 0), 1)],
-        2: [((1, 1), 0), ((1, 3), 0), ((1, 1), 1), ((1, 3), 1)],
-        3: [((3, 0), 0), ((3, 0), 1)],
-        4: [((1, 2),)],
+        1: [((3, 0), 0)],
+        2: [((3, 0), 1)],
+        3: [((1, 1), 0), ((1, 3), 0), ((1, 3), 1), ((1, 1), 1)],
+        4: [((4, 0), 0), ((2, 1), 0), ((4, 0), 1)],
+        5: [((2, 3), 0)],
+        6: [((2, 3), 1), ((2, 1), 1)],
+        7: [((1, 2), 0), ((3, 3), 0)],
+        8: [((3, 1), 0), ((3, 3), 1), ((3, 1), 1), ((1, 2), 1)],
     }
     pair_events = {
-        0: [((2, 1),), ((2, 3),), ((4, 0),)],
-        1: [((2, 2),)],
-        2: [((3, 1),), ((3, 3),)],
-        3: [((3, 2),), ((None, 1),)],
-        4: [((None, 3),), ((None, 2),)],
-        5: [],
+        0: [((2, 2), 0), ((2, 2), 1)],
+        1: [((None, 1),), ((3, 2), 0), ((3, 2), 1)],
+        2: [((None, 3),), ((None, 2),)],
+        3: [],
     }
     singles = len(single_events)
 

time: 42.6 us -> 40.8 us (0.958)
  Pallas kernels: 40.3 us -> 38.7 us
    pallas_call x1, Pallas kernels: 40.3 us -> 38.7 us  [per_device(): pl.pallas_call(attention_kernel, out_shape=jax.ShapeDtypeStruct((SHARD, L...]
where the time goes in v3:
time: 40.8 us; the launch traced here: 40.6 us
  Pallas kernels  38.7 us (95%)
  local copies, waits for them, and re-layouts  1.87 us (5%)
    pallas_call x1, Pallas kernels, per_device(): pl.pallas_call(attention_kernel, out_shape=jax.ShapeDtypeStruct((SHARD, L...  38.7 us
    unnamed x1, local copies, waits for them, and re-layouts  1.87 us

profile of v3, /device:TPU:504, one launch (start us, length us, event | category | flops | bytes accessed | tf_op | source)
XLA Modules:
  0.0 40.6 jit_solution(12027312633223001989)
XLA Ops:
  0.0 38.7 %shard_map.73 = bf16[512,512]{1,0:T(8,128)(2,1)} custom-call(bf16[512,512]{1,0:T(8,128)(2,1)} %query_hbm.1, bf16[512,128]{1,0:T(8,128)(2,1)} %key_value_hbm.1, f32[256,256]{1,0:T(8,128)} %constant.4.clone.row_table_hbm, f32[128]{0:T(128)} %query_gain_hbm.1, f32[128]{0:T(128)} %key_gain_hbm.1, s32[65]{0:T(128)} %offsets_hbm.1, ...), custom_call_target="tpu_custom_call" | custom-call | flops 8858370048 | bytes 2097152 | tf_op jit(solution)/shard_map/pallas_call | solution.py:467
  38.7 1.9 %copy.9 = bf16[512,512]{1,0:T(8,128)(2,1)} copy(bf16[512,512]{1,0:T(8,128)(2,1)} %shard_map.73) | data formatting | bytes 1048576

commit v4 on v3

--- a/solution.py
+++ b/solution.py
@@ -24,25 +24,26 @@
     (0, 0),
     (1, 0),
     (2, 0),
+    (1, 3),
     (3, 0),
     (1, 1),
-    (1, 3),
     (4, 0),
     (2, 3),
+    (3, 3),
+    (1, 2),
     (2, 1),
-    (1, 2),
-    (3, 3),
+    (None, 3),
+    (2, 2),
     (3, 1),
-    (2, 2),
     (None, 1),
     (3, 2),
-    (None, 3),
     (None, 2),
 ]
-EARLY = [((1, 0), 0), ((1, 0), 1), ((2, 0), 0), ((2, 0), 1)]
-ALONG_Z = ((3, 2), (2, 2), (3, 1))
+EARLY = [((1, 0), 0), ((1, 0), 1)]
+ALONG_Z = ((3, 1), (3, 3), (2, 2), (3, 2))
 SLOT = {place: index for index, place in enumerate(ORDER)}
 SLOTS = len(ORDER)
+PARTS = 2
 
 
 def rope_tables():
@@ -78,7 +79,6 @@
     local_sem,
     send_sem,
     recv_sem,
-    half_sem,
     pair_send_sem,
     pair_recv_sem,
 ):
@@ -175,10 +175,10 @@
         turned = wide * gained[0] + pltpu.roll(wide, HD // 2, 1) * gained[1]
         return (turned * factor).astype(jnp.bfloat16)
 
-    def rows_of(slot, half=None):
-        if half is None:
+    def rows_of(slot, part=None):
+        if part is None:
             return pl.ds(slot * SHARD, SHARD)
-        return pl.ds(slot * SHARD + half * UNIT, UNIT)
+        return pl.ds(slot * SHARD + part * (SHARD // PARTS), SHARD // PARTS)
 
     def holds(slot):
         row, step = ORDER[slot]
@@ -186,13 +186,12 @@
             return jnp.logical_or(x >= step, z >= 4)
         return z >= row
 
-    def to_chip(source, target, device, sem, half=None):
-        arrival = half_sem.at[target] if half == 1 else recv_sem.at[target]
+    def to_chip(source, target, device, sem, part=None):
         return pltpu.make_async_remote_copy(
-            src_ref=blocks.at[core, rows_of(source, half)],
-            dst_ref=blocks.at[core, rows_of(target, half)],
+            src_ref=blocks.at[core, rows_of(source, part)],
+            dst_ref=blocks.at[core, rows_of(target, part)],
             send_sem=send_sem.at[sem],
-            recv_sem=arrival,
+            recv_sem=recv_sem.at[target * PARTS + (part or 0)],
             device_id=device,
             device_id_type=pl.DeviceIdType.MESH,
         )
@@ -219,60 +218,69 @@
 
     sends = []
 
-    def plan(source, target, device, half, condition):
-        sends.append((source, target, device, half, condition))
+    def plan(source, target, device, part, condition):
+        sends.append((source, target, device, part, condition))
 
     ahead = {1: x_next, 2: x_across, 3: x_last}
     below = z < Z_SIZE - 1
-    for half in range(2):
-        plan(OWN, SLOT[(1, 0)], z_next, half, below)
+    for part in range(PARTS):
+        plan(OWN, SLOT[(1, 0)], z_next, part, below)
     for step in (1, 3, 2):
         plan(OWN, SLOT[(None, step)], ahead[step], None, x + step < X_SIZE)
     for row in (1, 2, 3):
         have = z >= row
         slot = SLOT[(row, 0)]
-        for half in range(2):
-            plan(slot, SLOT[(row + 1, 0)], z_next, half, jnp.logical_and(have, below))
+        for part in range(PARTS):
+            plan(slot, SLOT[(row + 1, 0)], z_next, part, jnp.logical_and(have, below))
             if (row, 1) not in ALONG_Z:
-                plan(slot, SLOT[(row, 1)], x_next, half, have)
+                plan(slot, SLOT[(row, 1)], x_next, part, have)
             if (row, 3) not in ALONG_Z:
-                plan(slot, SLOT[(row, 3)], x_last, half, have)
+                plan(slot, SLOT[(row, 3)], x_last, part, have)
             for step in (1, 2, 3):
                 if (row + 1, step) in ALONG_Z:
                     target = SLOT[(row + 1, step)]
-                    plan(SLOT[(row, step)], target, z_next, half, jnp.logical_and(have, below))
-        if (row, 2) not in ALONG_Z:
-            plan(SLOT[(row, 1)], SLOT[(row, 2)], x_next, 0, have)
-            plan(SLOT[(row, 3)], SLOT[(row, 2)], x_last, 1, have)
+                    plan(SLOT[(row, step)], target, z_next, part, jnp.logical_and(have, below))
+            if (row, 2) not in ALONG_Z:
+                if part < PARTS // 2:
+                    plan(SLOT[(row, 1)], SLOT[(row, 2)], x_next, part, have)
+                else:
+                    plan(SLOT[(row, 3)], SLOT[(row, 2)], x_last, part, have)
     for step in (1, 3, 2):
         condition = jnp.logical_and(x + step >= X_SIZE, z >= 4)
         plan(SLOT[(4, 0)], SLOT[(None, step)], ahead[step], None, condition)
 
-    def send_from(slot, halves):
-        for sem, (source, target, device, half, condition) in enumerate(sends):
-            if source == slot and half in halves:
+    def send_from(slot, parts):
+        for sem, (source, target, device, part, condition) in enumerate(sends):
+            if source == slot and part in parts:
 
                 @pl.when(condition)
                 def _():
-                    to_chip(source, target, device, sem, half).start()
+                    to_chip(source, target, device, sem, part).start()
 
     def arrived(place, half=None):
         slot = SLOT[place]
         if place[0] is None:
-            halves = (None,)
-        elif half is None:
-            halves = (0, 1)
+            parts = (None,)
         else:
-            halves = (half,)
-
-        @pl.when(holds(slot))
-        def _():
-            for part in halves:
+            parts = tuple(range(half * PARTS // 2, (half + 1) * PARTS // 2))
+        whole = parts[-1] in (None, PARTS - 1)
+
+        for part in parts:
+
+            @pl.when(holds(slot))
+            def _():
                 to_chip(slot, slot, x_next, 0, part).wait_recv()
-            if halves[-1] != 0:
-                to_partner(slot).start()
-
-        send_from(slot, halves + (None,) if halves[-1] == 1 else halves)
+
+            if part == parts[-1] and whole:
+
+                @pl.when(holds(slot))
+                def _():
+                    to_partner(slot).start()
+
+            if part is not None:
+                send_from(slot, (part,))
+        if whole and place[0] is not None:
+            send_from(slot, (None,))
 
     def wait_partner(slot):
         @pl.when(holds(slot))
@@ -300,9 +308,9 @@
         barrier, 4 + jnp.where(z > 0, 1, 0) + jnp.where(z < Z_SIZE - 1, 1, 0)
     )
 
-    send_from(OWN, (0,))
+    send_from(OWN, tuple(range(PARTS // 2)))
     prepare_keys(1)
-    send_from(OWN, (1,))
+    send_from(OWN, tuple(range(PARTS // 2, PARTS)))
     to_partner(OWN).start()
     send_from(OWN, (None,))
 
@@ -401,19 +409,19 @@
             held = later
 
     single_events = {
-        1: [((3, 0), 0)],
-        2: [((3, 0), 1)],
-        3: [((1, 1), 0), ((1, 3), 0), ((1, 3), 1), ((1, 1), 1)],
-        4: [((4, 0), 0), ((2, 1), 0), ((4, 0), 1)],
-        5: [((2, 3), 0)],
-        6: [((2, 3), 1), ((2, 1), 1)],
-        7: [((1, 2), 0), ((3, 3), 0)],
-        8: [((3, 1), 0), ((3, 3), 1), ((3, 1), 1), ((1, 2), 1)],
+        1: [((2, 0), 0), ((2, 0), 1)],
+        2: [((1, 3), 0), ((3, 0), 0), ((1, 3), 1), ((3, 0), 1), ((1, 1), 0)],
+        3: [((1, 1), 1), ((4, 0), 0), ((2, 3), 0)],
+        4: [((4, 0), 1), ((2, 1), 0)],
+        5: [((2, 3), 1)],
+        6: [((1, 2), 0), ((1, 2), 1)],
+        7: [((3, 3), 0), ((3, 1), 0), ((2, 1), 1), ((3, 3), 1)],
+        8: [((2, 2), 0)],
     }
     pair_events = {
-        0: [((2, 2), 0), ((2, 2), 1)],
-        1: [((None, 1),), ((3, 2), 0), ((3, 2), 1)],
-        2: [((None, 3),), ((None, 2),)],
+        0: [((2, 2), 1), ((None, 3),)],
+        1: [((None, 2),), ((3, 1), 1), ((None, 1),), ((3, 2), 0)],
+        2: [((3, 2), 1)],
         3: [],
     }
     singles = len(single_events)
@@ -428,16 +436,32 @@
                 for place in range(width):
                     wait_partner(first + width * index + place)
 
+    def needed(step, events, first, width):
+        found = False
+        for index in events:
+            slots = [first + width * index + place for place in range(width)]
+            exists = functools.reduce(jnp.logical_or, [holds(slot) for slot in slots])
+            found = jnp.logical_or(found, jnp.logical_and(step == index, exists))
+        return found
+
     def single(step, carry):
         take(step, single_events, 0, 1)
-        attend(step, 1)
+
+        @pl.when(needed(step, single_events, 0, 1))
+        def _():
+            attend(step, 1)
+
         return carry
 
     lax.fori_loop(1, 1 + singles, single, 0)
 
     def pair(step, carry):
         take(step, pair_events, 1 + singles, 2)
-        attend(1 + singles + 2 * step, 2)
+
+        @pl.when(needed(step, pair_events, 1 + singles, 2))
+        def _():
+            attend(1 + singles + 2 * step, 2)
+
         return carry
 
     lax.fori_loop(0, len(pair_events), pair, 0)
@@ -449,11 +473,11 @@
                 totals[unit, rows, :HD] / totals[unit, rows, HD:]
             ).astype(jnp.bfloat16)
 
-    for sem, (source, target, device, half, condition) in enumerate(sends):
+    for sem, (source, target, device, part, condition) in enumerate(sends):
 
         @pl.when(condition)
         def _():
-            to_chip(source, target, device, sem, half).wait_send()
+            to_chip(source, target, device, sem, part).wait_send()
 
     for slot in range(SLOTS):
 
@@ -481,9 +505,8 @@
             pltpu.VMEM((UNITS, ROWS, 2 * HD), jnp.float32),
             pltpu.SMEM((SLOTS,), jnp.int32),
             pltpu.SemaphoreType.DMA((7,)),
-            pltpu.SemaphoreType.DMA((40,)),
-            pltpu.SemaphoreType.DMA((SLOTS,)),
-            pltpu.SemaphoreType.DMA((SLOTS,)),
+            pltpu.SemaphoreType.DMA((96,)),
+            pltpu.SemaphoreType.DMA((SLOTS * PARTS,)),
             pltpu.SemaphoreType.DMA((SLOTS,)),
             pltpu.SemaphoreType.DMA((SLOTS,)),
         ],

time: 40.8 us -> 40 us (0.980)
  Pallas kernels: 38.7 us -> 37.9 us
    pallas_call x1, Pallas kernels: 38.7 us -> 37.9 us  [per_device(): pl.pallas_call(attention_kernel, out_shape=jax.ShapeDtypeStruct((SHARD, L...]
where the time goes in v4:
time: 40 us; the launch traced here: 39.8 us
  Pallas kernels  37.9 us (95%)
  local copies, waits for them, and re-layouts  1.87 us (5%)
    pallas_call x1, Pallas kernels, per_device(): pl.pallas_call(attention_kernel, out_shape=jax.ShapeDtypeStruct((SHARD, L...  37.9 us
    unnamed x1, local copies, waits for them, and re-layouts  1.87 us

profile of v4, /device:TPU:504, one launch (start us, length us, event | category | flops | bytes accessed | tf_op | source)
XLA Modules:
  0.0 39.8 jit_solution(6963680897870953490)
XLA Ops:
  0.0 37.9 %shard_map.73 = bf16[512,512]{1,0:T(8,128)(2,1)} custom-call(bf16[512,512]{1,0:T(8,128)(2,1)} %query_hbm.1, bf16[512,128]{1,0:T(8,128)(2,1)} %key_value_hbm.1, f32[256,256]{1,0:T(8,128)} %constant.4.clone.row_table_hbm, f32[128]{0:T(128)} %query_gain_hbm.1, f32[128]{0:T(128)} %key_gain_hbm.1, s32[65]{0:T(128)} %offsets_hbm.1, ...), custom_call_target="tpu_custom_call" | custom-call | flops 8858370048 | bytes 2097152 | tf_op jit(solution)/shard_map/pallas_call | solution.py:491
  37.9 1.9 %copy.9 = bf16[512,512]{1,0:T(8,128)(2,1)} copy(bf16[512,512]{1,0:T(8,128)(2,1)} %shard_map.73) | data formatting | bytes 1048576

commit v5 on v4

--- a/solution.py
+++ b/solution.py
@@ -343,7 +343,7 @@
 
     own_first = ctx * UNITS
 
-    def attend_own():
+    def attend_own(own_unit):
         keys = blocks[0, : UNITS * UNIT, :]
         row = lax.broadcasted_iota(jnp.int32, (SHARD, HD), 0) // UNIT
         unit_of_key = own_first + row
@@ -355,7 +355,7 @@
             masked_values(blocks[1, :SHARD, :], unit_of_key >= doc_units[unit])
             for unit in range(UNITS)
         ]
-        parts = [(unit, part) for unit in range(UNITS) for part in range(LOCAL_HEADS)]
+        parts = [(own_unit, part) for part in range(LOCAL_HEADS)]
 
         def part_scores(unit, part):
             return scores(unit, part, UNIT, keys[: (unit + 1) * UNIT])
@@ -381,9 +381,9 @@
     prepare_queries(0)
     prepare_queries(1)
     from_partner(OWN).wait_recv()
-    for arrival in EARLY:
+    for unit, arrival in enumerate(EARLY):
+        attend_own(unit)
         arrived(*arrival)
-    attend_own()
 
     def attend(slot, width):
         count = width * SHARD
@@ -409,9 +409,9 @@
             held = later
 
     single_events = {
-        1: [((2, 0), 0), ((2, 0), 1)],
-        2: [((1, 3), 0), ((3, 0), 0), ((1, 3), 1), ((3, 0), 1), ((1, 1), 0)],
-        3: [((1, 1), 1), ((4, 0), 0), ((2, 3), 0)],
+        1: [],
+        2: [((2, 0), 0), ((2, 0), 1), ((1, 3), 0)],
+        3: [((3, 0), 0), ((1, 3), 1), ((3, 0), 1), ((1, 1), 0), ((1, 1), 1), ((4, 0), 0), ((2, 3), 0)],
         4: [((4, 0), 1), ((2, 1), 0)],
         5: [((2, 3), 1)],
         6: [((1, 2), 0), ((1, 2), 1)],

time: 40 us -> 40.1 us (level)
  no operation moved by 1% of the time
where the time goes in v5:
time: 40.1 us; the launch traced here: 39.8 us
  Pallas kernels  38 us (95%)
  local copies, waits for them, and re-layouts  1.87 us (5%)
    pallas_call x1, Pallas kernels, per_device(): pl.pallas_call(attention_kernel, out_shape=jax.ShapeDtypeStruct((SHARD, L...  38 us
    unnamed x1, local copies, waits for them, and re-layouts  1.87 us

profile of v5, /device:TPU:504, one launch (start us, length us, event | category | flops | bytes accessed | tf_op | source)
XLA Modules:
  0.0 39.8 jit_solution(17886872702830246999)
XLA Ops:
  0.0 38.0 %shard_map.73 = bf16[512,512]{1,0:T(8,128)(2,1)} custom-call(bf16[512,512]{1,0:T(8,128)(2,1)} %query_hbm.1, bf16[512,128]{1,0:T(8,128)(2,1)} %key_value_hbm.1, f32[256,256]{1,0:T(8,128)} %constant.4.clone.row_table_hbm, f32[128]{0:T(128)} %query_gain_hbm.1, f32[128]{0:T(128)} %key_gain_hbm.1, s32[65]{0:T(128)} %offsets_hbm.1, ...), custom_call_target="tpu_custom_call" | custom-call | flops 8858370048 | bytes 2097152 | tf_op jit(solution)/shard_map/pallas_call | solution.py:491
  38.0 1.9 %copy.9 = bf16[512,512]{1,0:T(8,128)(2,1)} copy(bf16[512,512]{1,0:T(8,128)(2,1)} %shard_map.73) | data formatting | bytes 1048576
